TPU v7x, 512 devices: a whole 4x4x16 slice. The times are simulated.
512 devices in a mesh: src: 128 (over z, y, core), tgt: 4 (over x).
Axes of the slice: x: 4, y: 4, z: 16, core: 2. Of those that a mesh axis runs over, the one named last changes fastest.
Arguments:
- source_mean: float32 [16, 32768], P(None, 'src'), may hold values from -1 to 1, as said below
- target_points: float32 [16, 16384], P(None, 'tgt'), may hold values from -1 to 1
- precision: float32 [16], replicated, may hold values from 0.25 to 2, as said below
- target_values: float32 [16384, 128], P('tgt'), may hold values from 0.5 to 3
- cash: float32 [32768, 128], P('src'), may hold values from -3 to 3
- salvage: float32 [32768, 128], P('src'), may hold values from 0.5 to 3
- switch_cost: float32 [128], replicated, may hold values from 0.05 to 0.5
- cotangent: float32 [32768, 128], P('src'), may hold values from -0.5 to 1.5
- decision: int32 [32768, 128], P('src'), may hold values from 0 to 2
Outputs:
- source_value: float32 [32768, 128], P('src')
- target_adjoint: float32 [4, 4096, 128], P('tgt', 'src')
Inputs may be any that keep to these rules, and one draw needn't show every extreme that they name: `source_mean`: the first factor of source i lies between -1 + 2 i / 32768 and -1 + 2 (i + 1) / 32768. The first factor's precision is 1.5 or more.
All inputs are finite; a program needn't handle non-finite values.
Results may differ from a plain program's by a relative error of at most 0.00024.
Values sent between devices are 32-bit elements; how exact they have to be, the bound alone decides.
A program may use at most 64 MiB of HBM per device.

v0:
```python
import jax
import jax.numpy as jnp
from jax import lax
from jax.sharding import PartitionSpec as P


def choose_value(continuation, cash_part, salvage_part, cost_part):
    hold_value = continuation + cash_part
    paired = hold_value.reshape(hold_value.shape[0], -1, 2)[:, :, ::-1].reshape(hold_value.shape)
    switched = paired - cost_part[None, :]
    return jnp.maximum(jnp.maximum(hold_value, switched), salvage_part)


def adjoint_input(cotangent, decision):
    held = jnp.where(decision == 0, cotangent, 0.0)
    moved = jnp.where(decision == 1, cotangent, 0.0)
    swapped = moved.reshape(moved.shape[0], -1, 2)[:, :, ::-1].reshape(moved.shape)
    return held + swapped


def transposed_product(left_part, right_part):
    return lax.dot_general(
        left_part,
        right_part,
        (((0,), (0,)), ((), ())),
        precision=lax.Precision.HIGHEST,
        preferred_element_type=jnp.float32,
    )


def on_device(
    source_mean,
    target_points,
    precision,
    target_values,
    cash,
    salvage,
    switch_cost,
    cotangent,
    decision,
):
    source_total = source_mean.shape[1] * lax.axis_size("src")
    target_total = target_points.shape[1] * lax.axis_size("tgt")
    scaled = source_mean * precision[:, None]
    offset = -0.5 * jnp.sum(scaled * source_mean, axis=0)
    density = jnp.exp(transposed_product(scaled, target_points) + offset[:, None])
    column_sum = lax.psum(jnp.sum(density, axis=0), "src")
    factor = source_total / target_total / column_sum
    scaled_values = target_values * factor[:, None]
    partial_terms = jnp.dot(
        density, scaled_values, precision=lax.Precision.HIGHEST, preferred_element_type=jnp.float32
    )
    continuation = lax.psum(partial_terms, "tgt")
    source_value = choose_value(continuation, cash, salvage, switch_cost)
    adjoint_in = adjoint_input(cotangent, decision)
    row_count = target_points.shape[1] // lax.axis_size("src")
    weights = density * factor[None, :]
    weighted_terms = transposed_product(weights, adjoint_in)
    own_rows = lax.psum_scatter(weighted_terms, "src", scatter_dimension=0, tiled=True)
    target_adjoint = own_rows.reshape(1, row_count, own_rows.shape[1])
    return (source_value, target_adjoint)


def solution(mesh):
    placed = (
        P(None, "src"),
        P(None, "tgt"),
        P(),
        P("tgt", None),
        P("src", None),
        P("src", None),
        P(),
        P("src", None),
        P("src", None),
    )
    return jax.shard_map(
        on_device,
        mesh=mesh,
        in_specs=placed,
        out_specs=(P("src", None), P("tgt", "src", None)),
        check_vma=False,
    )
```

profile of v0, /device:TPU:1, one launch (start us, length us, event | category | flops | bytes accessed | tf_op | source)
XLA Modules:
  0.0 786.9 jit_solution(16784682640421610554)
XLA Ops:
  8.0 0.0 copy-start
  8.0 0.0 copy-start.1
  8.0 0.0 all-reduce.2.cloned.1.call-start
  8.1 1.0 fusion.13
  9.0 0.0 copy-done
  9.0 6.3 fusion.17
  15.4 0.0 copy-start.4
  15.4 0.0 copy-start.5
  15.4 498.2 %psum.14 = f32[4096]{0:T(1024)S(1)} all-reduce(f32[4096]{0:T(1024)S(1)} %get-tuple-element.2), channel_id=1, replica_groups=mesh['src'=128,'tgt'=4] {'src'}, use_global_device_ids=true, to_apply=%region_2.0 | all-reduce | flops 4096 | bytes 32768 | tf_op jit(solution)/shard_map/psum | solution.py:47
  513.6 0.0 copy-done.1
  513.6 6.4 fusion.4
  519.9 0.0 all-reduce.2.cloned.1.call-update
  520.0 0.2 reduce-scatter.2.cloned.1.call-start
  520.2 0.0 copy-done.4
  520.2 0.1 copy.14
  520.3 0.0 copy-done.5
  520.3 0.1 copy.13
  520.4 0.1 reshape.28
  520.5 0.4 rev.7
  520.9 0.1 reshape.29
  521.0 0.0 copy-start.2
  521.0 0.0 copy-start.3
  521.0 0.0 copy-start.6
  521.1 10.3 %fusion.1 = f32[4096,128]{1,0:T(8,128)} fusion(f32[256,4096]{1,0:T(8,128)} %get-tuple-element.3, f32[4096]{0:T(1024)S(1)} %broadcast_divide_fusion, f32[256,128]{0,1:T(8,128)S(1)} %reshape.29, f32[256,128]{0,1:T(8,128)S(1)} %copy.14, s32[256,128]{0,1:T(8,128)S(1)} %copy.13), kind=kOutput, calls=%fused_computation.2 | convolution fusion | flops 1611759616 | bytes 6701056 | tf_op jit(solution)/shard_map/dot_general | solution.py:22
  531.3 0.0 reduce-scatter.2.cloned.1.call-update
  531.3 40.8 %all-reduce.2.cloned.1.call-done = f32[256,128]{1,0:T(8,128)} async-done(((f32[256,128]{1,0:T(8,128)}), f32[256,128]{1,0:T(8,128)}) %all-reduce.2.cloned.1.call-update) | async-done | bytes 131088 | tf_op jit(solution)/shard_map/psum | solution.py:53
  572.1 0.0 copy-done.2
  572.1 0.9 add.22
  573.0 0.1 copy.11
  573.1 0.1 reshape.26
  573.2 0.4 rev.6
  573.6 0.1 reshape.27
  573.7 0.1 copy.12
  573.8 0.0 copy-done.3
  573.8 0.0 copy-done.6
  573.8 0.7 maximum_maximum_fusion
  574.5 204.9 %reduce-scatter.2.cloned.1.call-done = f32[32,128]{1,0:T(8,128)} async-done(((f32[4096,128]{1,0:T(8,128)}), f32[32,128]{1,0:T(8,128)}) %reduce-scatter.2.cloned.1.call-update) | async-done | bytes 16400 | tf_op jit(solution)/shard_map/reduce_scatter | solution.py:59
  (3 shorter events, 0.0 us)
Async XLA Ops:
  8.0 1.0 copy-start
  8.0 505.6 %copy-start.1 = (f32[4096,128]{1,0:T(8,128)S(1)}, f32[4096,128]{1,0:T(8,128)}, u32[]{:S(2)}) copy-start(f32[4096,128]{1,0:T(8,128)} %param.12) | copy-start | bytes 6291460
  8.0 564.1 %all-reduce.2.cloned.1.call-start = ((), (), s32[]{:S(2)}) async-start(), calls=%async_computation.1 | async-start | bytes 262144 | tf_op jit(solution)/shard_map/psum | solution.py:53
  15.4 504.8 %copy-start.4 = (f32[256,128]{1,0:T(8,128)S(1)}, f32[256,128]{1,0:T(8,128)}, u32[]{:S(2)}) copy-start(f32[256,128]{1,0:T(8,128)} %param.16) | copy-start | bytes 393220
  15.4 504.9 %copy-start.5 = (s32[256,128]{1,0:T(8,128)S(1)}, s32[256,128]{1,0:T(8,128)}, u32[]{:S(2)}) copy-start(s32[256,128]{1,0:T(8,128)} %param.17) | copy-start | bytes 393220
  520.0 259.5 %reduce-scatter.2.cloned.1.call-start = ((), (), s32[]{:S(2)}) async-start(), calls=%async_computation.2 | async-start | bytes 2113536 | tf_op jit(solution)/shard_map/reduce_scatter | solution.py:59
  521.0 51.1 %copy-start.2 = (f32[256,128]{1,0:T(8,128)S(1)}, f32[256,128]{1,0:T(8,128)}, u32[]{:S(2)}) copy-start(f32[256,128]{1,0:T(8,128)} %param.13) | copy-start | bytes 393220
  521.0 52.8 %copy-start.3 = (f32[256,128]{1,0:T(8,128)S(1)}, f32[256,128]{1,0:T(8,128)}, u32[]{:S(2)}) copy-start(f32[256,128]{1,0:T(8,128)} %param.14) | copy-start | bytes 393220
  521.0 52.8 %copy-start.6 = (f32[128]{0:T(128)S(1)}, f32[128]{0:T(128)}, u32[]{:S(2)}) copy-start(f32[128]{0:T(128)} %param.15) | copy-start | bytes 1540
Sparse Core Ops, SparseCore 0:
  520.1 51.9 all-reduce.1
Sparse Core Ops, SparseCore 1:
  531.4 247.9 reduce-scatter.1
where the time goes:
time: 797 us; the launch traced here: 787 us
  blocking collectives  498 us (62%)
  waiting for transfers between devices  246 us (31%)
  matrix products  22.9 us (3%)
  between operations  15.6 us (2%)
    psum x1, blocking collectives, on_device(): column_sum = lax.psum(jnp.sum(density, axis=0), 'src')  498 us
    reduce_scatter x1, waiting for transfers between devices, on_device(): lax.psum_scatter(weighted_terms, 'src', scatter_dimension=0, tiled=True)  205 us
    psum x1, waiting for transfers between devices, on_device(): continuation = lax.psum(partial_terms, 'tgt')  40.8 us
    dot_general x2, matrix products, transposed_product(): lax.dot_general(left_part, right_part, (((0,), (0,)), ((), ())), precisio...  16.6 us
  transfers between devices with their start and end apart: 2, of which 2 were waited for; matrix products, arithmetic and copies ran while one was open for 2% of the time, Pallas kernels for 0%

commit v1 on v0

v1 whole, which is shorter than its diff:
```python
import functools
import math

import jax
import jax.numpy as jnp
from jax import lax
from jax.experimental import pallas as pl
from jax.experimental.pallas import tpu as pltpu
from jax.sharding import PartitionSpec as P

F32, BF16 = jnp.float32, jnp.bfloat16
MESH = pl.DeviceIdType.MESH
LOG2E = math.log2(math.e)


def split2(v):
    hi = v.astype(BF16)
    return hi, (v - hi.astype(F32)).astype(BF16)


def split3(v):
    hi = v.astype(BF16)
    rest = v - hi.astype(F32)
    mid = rest.astype(BF16)
    return hi, mid, (rest - mid.astype(F32)).astype(BF16)


def beside(v):
    hi, lo = split2(v)
    return jnp.concatenate([hi, lo], axis=1)


def source_stack(mean, prec_col):
    scaled = mean * prec_col
    offset = jnp.sum(scaled * mean, axis=0, keepdims=True) * (-0.5 * LOG2E)
    a, b, c = split3(scaled * LOG2E)
    p, q, r = split3(offset)
    row = lax.broadcasted_iota(jnp.int32, mean.shape, 0)
    tail = jnp.where(
        row == 0, p.astype(F32), jnp.where(row == 1, q.astype(F32), jnp.where(row == 2, r.astype(F32), 0.0))
    ).astype(BF16)
    return jnp.concatenate([a, a, b, a, b, c, tail], axis=0)


def target_stack(points):
    a, b, c = split3(points)
    row = lax.broadcasted_iota(jnp.int32, points.shape, 0)
    tail = jnp.where(row < 3, 1.0, 0.0).astype(BF16)
    return jnp.concatenate([a, b, a, c, b, a, tail], axis=0)


def pair_swap(v):
    lane = lax.broadcasted_iota(jnp.int32, v.shape, 1)
    width = v.shape[1]
    return jnp.where(lane % 2 == 0, pltpu.roll(v, width - 1, 1), pltpu.roll(v, 1, 1))


def tdot(a, b):
    return lax.dot_general(a, b, (((0,), (0,)), ((), ())), preferred_element_type=F32)


def dot(a, b):
    return jnp.dot(a, b, preferred_element_type=F32)


def kernel(
    dims,
    scale,
    mean_h, points_h, prec_s, values_h, cash_h, salvage_h, cost_v, cot_h, dec_h,
    value_out, adjoint_out,
    mean_v, adj, cot_v, dec_v, points_v, values_v, cash_v, salvage_v,
    dens, sstack, tstack, t2, vstack, acc,
    colpart, rs_buf, zc_src, zc_buf, col_all,
    sib_src, sib_buf, zb_src, zb_buf,
    xr_src, xr_buf, value_v,
    ld_sem, g_send, g_recv, rs_send, rs_recv, zc_send, zc_recv, ag_send, ag_recv,
    sib_send, sib_recv, zb_send, zb_recv, xr_send, xr_recv, xa_send, xa_recv,
):
    Z, Y, C, X = dims
    W = Y * C
    S, M = cot_v.shape
    T = points_v.shape[1]
    TW = T // W
    R = T // (Z * W)
    S4 = S // X
    s = lax.axis_index("src")
    x = lax.axis_index("tgt")
    z, w = s // W, s % W
    y, c = w // C, w % C

    def at_z(i):
        return (((z + i) % Z) * W + w, x)

    def at_w(i):
        return (z * W + (w + i) % W, x)

    def at_y(i):
        return (z * W + ((y + i) % Y) * C + c, x)

    def at_x(i):
        return (s, (x + i) % X)

    sibling = (z * W + y * C + (1 - c), x)

    def remote(src, dst, send, recv, dev):
        cp = pltpu.make_async_remote_copy(
            src_ref=src, dst_ref=dst, send_sem=send, recv_sem=recv, device_id=dev, device_id_type=MESH
        )
        cp.start()
        return cp

    def near_far(n):
        return sorted(range(1, n), key=lambda i: -min(i, n - i))

    loads = {}
    for k, (name, src, dst) in enumerate([
        ("cot", cot_h, cot_v), ("dec", dec_h, dec_v), ("mean", mean_h, mean_v.at[0]), ("points", points_h, points_v),
        ("values", values_h, values_v), ("cash", cash_h, cash_v), ("salvage", salvage_h, salvage_v),
    ]):
        loads[name] = pltpu.make_async_copy(src, dst, ld_sem.at[k])
        loads[name].start()

    barrier = pltpu.get_barrier_semaphore()
    peers = [at_w(i) for i in range(1, W)] + [at_z(i) for i in range(1, Z)] + [at_x(i) for i in range(1, X)]
    for dev in peers:
        pl.semaphore_signal(barrier, inc=1, device_id=dev, device_id_type=MESH)

    loads["cot"].wait()
    loads["dec"].wait()
    cot = cot_v[...]
    dec = dec_v[...]
    adj[0] = jnp.where(dec == 0, cot, 0.0) + pair_swap(jnp.where(dec == 1, cot, 0.0))
    loads["mean"].wait()
    frow = lax.broadcasted_iota(jnp.int32, (mean_v.shape[1], 1), 0)
    prec_col = jnp.zeros((mean_v.shape[1], 1), F32)
    for f in range(mean_v.shape[1]):
        prec_col = jnp.where(frow == f, prec_s[f], prec_col)

    pl.semaphore_wait(barrier, len(peers))

    sends = []
    gathers = {}
    for i in sorted(range(1, Y), key=lambda i: min(i, Y - i)):
        gathers[i] = [
            remote(mean_v.at[0], mean_v.at[i], g_send.at[i, 0], g_recv.at[i, 0], at_y(i)),
            remote(adj.at[0], adj.at[i], g_send.at[i, 1], g_recv.at[i, 1], at_y(i)),
        ]
        sends += gathers[i]

    sstack[0] = source_stack(mean_v[0], prec_col)
    loads["points"].wait()

    def first_density(j, carry):
        cols = pl.ds(pl.multiple_of(j * TW, TW), TW)
        tstack_j = target_stack(points_v[:, cols])
        d = jnp.exp2(tdot(sstack[0], tstack_j))
        dens[:, cols] = d
        colpart[j] = jnp.sum(d, axis=0, keepdims=True)
        return carry

    lax.fori_loop(0, W, first_density, 0)

    rs = []
    for i in range(1, W):
        rs.append(remote(colpart.at[(w + i) % W], rs_buf.at[i], rs_send.at[i], rs_recv.at[i], at_w(i)))
    sends += rs

    width = min(128, Z * R)
    lane = lax.broadcasted_iota(jnp.int32, (mean_v.shape[1], width), 1)
    per = width // R
    for half in range(2):
        core = (c + 1 + half) % C
        blocks = []
        for g in range(Z // per):
            block = jnp.zeros((mean_v.shape[1], width), F32)
            for k in range(per):
                off = (g * per + k) * (W * R) + (y * C + core) * R
                base = pl.multiple_of(off // width * width, width)
                turn = (k * R + width - off % width) % width
                piece = pltpu.roll(points_v[:, pl.ds(base, width)], turn, 1)
                block = jnp.where((lane >= k * R) & (lane < (k + 1) * R), piece, block)
            blocks.append(block)
        t2[half] = target_stack(jnp.concatenate(blocks, axis=1))

    for cp in rs:
        cp.wait_recv()
    total = colpart[w]
    for i in range(1, W):
        total = total + rs_buf[i]
    zc_src[...] = total
    zc_buf[0] = total
    zc = []
    for i in near_far(Z):
        zc.append(remote(zc_src, zc_buf.at[i], zc_send.at[i], zc_recv.at[i], at_z(i)))
    sends += zc

    def back_block(i, half, first):
        d = jnp.exp2(tdot(t2[half], sstack[i]))
        hi, lo = split2(d)
        a = beside(adj[i])
        term = dot(hi, a) + dot(lo, a)
        acc[half] = term if first else acc[half] + term

    back_block(0, 0, True)
    back_block(0, 1, True)

    loads["values"].wait()

    def stack_values(j, carry):
        rows = pl.ds(pl.multiple_of(j * TW, TW), TW)
        vstack[rows, :] = beside(values_v[rows, :])
        return carry

    lax.fori_loop(0, W, stack_values, 0)

    for cp in zc:
        cp.wait_recv()
    total = zc_buf[0]
    for i in range(1, Z):
        total = total + zc_buf[i]
    col_all[w] = total
    ag = []
    for i in range(1, W):
        ag.append(remote(col_all.at[w], col_all.at[w], ag_send.at[i], ag_recv.at[i], at_w(i)))
    sends += ag

    order = sorted(range(1, Y), key=lambda i: min(i, Y - i))
    for n, i in enumerate(order):
        for cp in gathers[i]:
            cp.wait_recv()
        sstack[i] = source_stack(mean_v[i], prec_col)
        back_block(i, 0, False)
        if n == len(order) - 1:
            sib_src[...] = acc[0, :, :M] + acc[0, :, M:]
            sib = remote(sib_src, sib_buf, sib_send, sib_recv, sibling)
            sends.append(sib)
        back_block(i, 1, False)

    own = acc[1, :, :M] + acc[1, :, M:]
    sib.wait_recv()
    own = own + sib_buf[...]
    zb_src[...] = own.reshape(Z, R, M)
    zb = []
    for i in near_far(Z):
        zb.append(remote(zb_src.at[(z + i) % Z], zb_buf.at[i], zb_send.at[i], zb_recv.at[i], at_z(i)))
    sends += zb

    for cp in ag:
        cp.wait_recv()

    def forward(j, total):
        cols = pl.ds(pl.multiple_of(j * TW, TW), TW)
        hi, lo = split2(dens[:, cols] * (scale / col_all[j]))
        v = vstack[cols, :]
        return total + dot(hi, v) + dot(lo, v)

    both = lax.fori_loop(0, W, forward, jnp.zeros((S, 2 * M), F32))
    xr_src[...] = (both[:, :M] + both[:, M:]).reshape(X, S4, M)
    xr = []
    for i in near_far(X):
        xr.append(remote(xr_src.at[(x + i) % X], xr_buf.at[i], xr_send.at[i], xr_recv.at[i], at_x(i)))
    sends += xr
    loads["cash"].wait()
    loads["salvage"].wait()
    for cp in xr:
        cp.wait_recv()
    rows = pl.ds(pl.multiple_of(x * S4, S4), S4)
    hold = xr_src[x]
    for i in range(1, X):
        hold = hold + xr_buf[i]
    hold = hold + cash_v[rows, :]
    value_v[x] = jnp.maximum(jnp.maximum(hold, pair_swap(hold) - cost_v[...]), salvage_v[rows, :])
    xa = []
    for i in near_far(X):
        xa.append(remote(value_v.at[x], value_v.at[x], xa_send.at[i], xa_recv.at[i], at_x(i)))
    sends += xa

    own_off = s * R
    jw = own_off // TW
    inner = own_off % TW
    win = min(128, TW)
    base = pl.multiple_of(inner // win * win, win)
    line = col_all[jw, :, pl.ds(base, win)]
    r_iota = lax.broadcasted_iota(jnp.int32, (R, win), 0)
    l_iota = lax.broadcasted_iota(jnp.int32, (R, win), 1)
    own_sum = jnp.sum(jnp.where(l_iota == r_iota + inner % win, line, 0.0), axis=1, keepdims=True)
    own_factor = scale / own_sum

    for cp in zb:
        cp.wait_recv()
    raw = zb_src[z]
    for i in range(1, Z):
        raw = raw + zb_buf[i]
    adjoint_out[0] = raw * own_factor

    for cp in xa:
        cp.wait_recv()
    value_out[...] = value_v[...].reshape(S, M)
    for cp in sends:
        cp.wait_send()


def on_device(dims, mean, points, precision, values, cash, salvage, cost, cot, dec):
    Z, Y, C, X = dims
    W = Y * C
    F, S = mean.shape
    T = points.shape[1]
    M = cot.shape[1]
    R, TW, K = T // (Z * W), T // W, 7 * F
    scale = float(S * Z * W) / float(T * X)
    hbm = pl.BlockSpec(memory_space=pltpu.HBM)
    vmem = pl.BlockSpec(memory_space=pltpu.VMEM)
    dma = pltpu.SemaphoreType.DMA
    scratch = [
        pltpu.VMEM((Y, F, S), F32), pltpu.VMEM((Y, S, M), F32), pltpu.VMEM((S, M), F32), pltpu.VMEM((S, M), jnp.int32),
        pltpu.VMEM((F, T), F32), pltpu.VMEM((T, M), F32), pltpu.VMEM((S, M), F32), pltpu.VMEM((S, M), F32),
        pltpu.VMEM((S, T), F32), pltpu.VMEM((Y, K, S), BF16), pltpu.VMEM((16, 128), BF16), pltpu.VMEM((2, K, Z * R), BF16),
        pltpu.VMEM((T, 2 * M), BF16), pltpu.VMEM((2, Z * R, 2 * M), F32),
        pltpu.VMEM((W, 1, TW), F32), pltpu.VMEM((W, 1, TW), F32), pltpu.VMEM((1, TW), F32), pltpu.VMEM((Z, 1, TW), F32),
        pltpu.VMEM((W, 1, TW), F32),
        pltpu.VMEM((Z * R, M), F32), pltpu.VMEM((Z * R, M), F32), pltpu.VMEM((Z, R, M), F32), pltpu.VMEM((Z, R, M), F32),
        pltpu.VMEM((X, S // X, M), F32), pltpu.VMEM((X, S // X, M), F32), pltpu.VMEM((X, S // X, M), F32),
        dma((7,)), dma((Y, 2)), dma((Y, 2)), dma((W,)), dma((W,)), dma((Z,)), dma((Z,)), dma((W,)), dma((W,)),
        dma, dma, dma((Z,)), dma((Z,)), dma((X,)), dma((X,)), dma((X,)), dma((X,)),
    ]
    return pl.pallas_call(
        functools.partial(kernel, dims, scale),
        out_shape=(jax.ShapeDtypeStruct((S, M), F32), jax.ShapeDtypeStruct((1, R, M), F32)),
        in_specs=[hbm, hbm, pl.BlockSpec(memory_space=pltpu.SMEM), hbm, hbm, hbm, vmem, hbm, hbm],
        out_specs=(vmem, vmem),
        scratch_shapes=scratch,
        compiler_params=pltpu.CompilerParams(
            collective_id=0, has_side_effects=True, vmem_limit_bytes=60 * 1024 * 1024
        ),
        name="mesh_step",
    )(mean, points, precision, values, cash, salvage, cost.reshape(1, M), cot, dec)


def build(mesh, dims):
    placed = (
        P(None, "src"), P(None, "tgt"), P(), P("tgt", None), P("src", None), P("src", None), P(), P("src", None),
        P("src", None),
    )
    return jax.shard_map(
        functools.partial(on_device, dims),
        mesh=mesh,
        in_specs=placed,
        out_specs=(P("src", None), P("tgt", "src", None)),
        check_vma=False,
    )


def solution(mesh):
    src, tgt = mesh.shape["src"], mesh.shape["tgt"]
    return build(mesh, (src // 8, 4, 2, tgt))
```

time: 797 us -> 55.4 us (0.07); the launches traced: 787 us -> 55.2 us
  blocking collectives: 498 us -> 0 us
  waiting for transfers between devices: 246 us -> 0 us
  Pallas kernels: 0 us -> 51.7 us
  matrix products: 22.9 us -> 0 us
  between operations: 15.6 us -> 0.64 us
    psum x1 -> x0, blocking collectives: 498 us -> none  [on_device(): column_sum = lax.psum(jnp.sum(density, axis=0), 'src')]
    reduce_scatter x1 -> x0, waiting for transfers between devices: 205 us -> none  [on_device(): lax.psum_scatter(weighted_terms, 'src', scatter_dimension=0, tiled=True)]
    pallas_call x0 -> x1, Pallas kernels: none -> 51.7 us  [on_device(): pl.pallas_call(functools.partial(kernel, dims, scale), out_shape=(jax.Sha...]
    psum x1 -> x0, waiting for transfers between devices: 40.8 us -> none  [on_device(): continuation = lax.psum(partial_terms, 'tgt')]
    dot_general x3 -> x0, matrix products: 23 us -> none  [the longest x2 16.6 us: transposed_product(): lax.dot_general(left_part, right_part, (((0,), (0,)), ((), ())), precisio...]
  transfers between devices with their start and end apart: 2 -> 0, of which waited for: 2 -> 0; matrix products, arithmetic and copies ran while one was open for 2% -> 0% of each run, Pallas kernels for 0% -> 0%
where the time goes in v1:
time: 55.4 us; the launch traced here: 55.2 us
  Pallas kernels  51.7 us (93%)
  local copies, waits for them, and re-layouts  2.89 us (5%)
  between operations  0.64 us (1%)
    pallas_call x1, Pallas kernels, on_device(): pl.pallas_call(functools.partial(kernel, dims, scale), out_shape=(jax.Sha...  51.7 us
    unnamed x2, local copies, waits for them, and re-layouts  2.89 us

profile of v1, /device:TPU:1, one launch (start us, length us, event | category | flops | bytes accessed | tf_op | source)
XLA Modules:
  0.0 55.2 jit_solution(1007347174910235633)
XLA Ops:
  0.6 51.7 %mesh_step.1 = (f32[256,128]{1,0:T(8,128)}, f32[1,32,128]{2,1,0:T(8,128)}) custom-call(f32[16,256]{1,0:T(8,128)} %mean_h.1, f32[16,4096]{1,0:T(8,128)} %points_h.1, f32[16]{0:T(128)} %prec_s.1, f32[4096,128]{1,0:T(8,128)} %values_h.1, f32[256,128]{1,0:T(8,128)} %cash_h.1, f32[256,128]{1,0:T(8,128)} %salvage_h.1, f32[1,128]{1,0:T(1,128)} %bitcast.1, ...), custom_call_target="tpu_custom_call" | custom-call | tf_op jit(solution)/shard_map/mesh_step/pallas_call | solution.py:326
  52.3 1.6 %copy.13 = f32[256,128]{1,0:T(8,128)} copy(f32[256,128]{1,0:T(8,128)} %get-tuple-element.4) | data formatting | bytes 262144
  53.9 1.3 %copy.14 = f32[1,32,128]{2,1,0:T(8,128)} copy(f32[1,32,128]{2,1,0:T(8,128)} %get-tuple-element.5) | data formatting | bytes 32768

commit v2 on v1

v2 whole, which is shorter than its diff:
```python
import functools
import math

import jax
import jax.numpy as jnp
from jax import lax
from jax.experimental import pallas as pl
from jax.experimental.pallas import tpu as pltpu
from jax.sharding import PartitionSpec as P

F32, BF16 = jnp.float32, jnp.bfloat16
MESH = pl.DeviceIdType.MESH
LOG2E = math.log2(math.e)


def split2(v):
    hi = v.astype(BF16)
    return hi, (v - hi.astype(F32)).astype(BF16)


def split3(v):
    hi = v.astype(BF16)
    rest = v - hi.astype(F32)
    mid = rest.astype(BF16)
    return hi, mid, (rest - mid.astype(F32)).astype(BF16)


def beside(v):
    hi, lo = split2(v)
    return jnp.concatenate([hi, lo], axis=1)


def source_stack(mean, prec_col):
    scaled = mean * prec_col
    offset = jnp.sum(scaled * mean, axis=0, keepdims=True) * (-0.5 * LOG2E)
    a, b, c = split3(scaled * LOG2E)
    p, q, r = split3(offset)
    row = lax.broadcasted_iota(jnp.int32, mean.shape, 0)
    tail = jnp.where(
        row == 0, p.astype(F32), jnp.where(row == 1, q.astype(F32), jnp.where(row == 2, r.astype(F32), 0.0))
    ).astype(BF16)
    return jnp.concatenate([a, a, b, a, b, c, tail], axis=0)


def target_stack(points):
    a, b, c = split3(points)
    row = lax.broadcasted_iota(jnp.int32, points.shape, 0)
    tail = jnp.where(row < 3, 1.0, 0.0).astype(BF16)
    return jnp.concatenate([a, b, a, c, b, a, tail], axis=0)


def pair_swap(v):
    lane = lax.broadcasted_iota(jnp.int32, v.shape, 1)
    width = v.shape[1]
    return jnp.where(lane % 2 == 0, pltpu.roll(v, width - 1, 1), pltpu.roll(v, 1, 1))


def tdot(a, b):
    return lax.dot_general(a, b, (((0,), (0,)), ((), ())), preferred_element_type=F32)


def dot(a, b):
    return jnp.dot(a, b, preferred_element_type=F32)


def kernel(
    dims,
    scale,
    mean_h, points_h, prec_h, values_h, cash_h, salvage_h, cost_h, cot_h, dec_h,
    value_out, adjoint_out,
    mean_v, adj, cot_v, dec_v, points_v, values_v, cash_v, salvage_v, prec_s, cost_v,
    dens, sstack, t2, vstack, acc,
    colpart, rs_buf, zc_src, zc_buf, col_all,
    sib_src, sib_buf, own_v, z_src, z1_buf, z2_src, z2_buf,
    xr_src, xr_buf, value_v,
    ld_sem, g_send, g_recv, rs_send, rs_recv, zc_send, zc_recv, ag_send, ag_recv,
    sib_send, sib_recv, z1_send, z1_recv, z2_send, z2_recv, xr_send, xr_recv, xa_send, xa_recv, far_sem,
):
    Z, Y, C, X = dims
    W = Y * C
    S, M = cot_v.shape
    F, T = points_v.shape
    TW = T // W
    R = T // (Z * W)
    S4 = S // X
    H = Z // 2
    NEAR = 4
    s = lax.axis_index("src")
    x = lax.axis_index("tgt")
    z, w = s // W, s % W
    y, c = w // C, w % C

    def at_z(i):
        return (((z + i + Z) % Z) * W + w, x)

    def place(i, k):
        return ((y + i) % Y) * C + (c + k) % C

    def at_w(i, k):
        return (z * W + place(i, k), x)

    def at_x(i):
        return (s, (x + i) % X)

    def remote(src, dst, send, recv, dev):
        cp = pltpu.make_async_remote_copy(
            src_ref=src, dst_ref=dst, send_sem=send, recv_sem=recv, device_id=dev, device_id_type=MESH
        )
        cp.start()
        return cp

    def far_first(n):
        return sorted(range(1, n), key=lambda i: -min(i, n - i))

    near_y = sorted(range(1, Y), key=lambda i: min(i, Y - i))
    plane = [(i, k) for i in reversed(near_y) for k in range(C)] + [(0, k) for k in range(1, C)]

    loads = {}

    def load(k, name, src, dst):
        loads[name] = pltpu.make_async_copy(src, dst, ld_sem.at[k])
        loads[name].start()

    load(0, "prec", prec_h, prec_s)
    load(1, "mean", mean_h, mean_v.at[0])
    load(2, "points", points_h, points_v)
    load(3, "cot", cot_h, cot_v)
    load(4, "dec", dec_h, dec_v)

    barrier = pltpu.get_barrier_semaphore()
    near_z = [i for i in far_first(Z) if min(i, Z - i) <= NEAR]
    peers = [at_z(i) for i in near_z] + [at_w(i, k) for i, k in plane] + [at_x(i) for i in far_first(X)]
    for dev in peers:
        pl.semaphore_signal(barrier, inc=1, device_id=dev, device_id_type=MESH)

    loads["prec"].wait()
    loads["mean"].wait()
    frow = lax.broadcasted_iota(jnp.int32, (F, 1), 0)
    prec_col = jnp.zeros((F, 1), F32)
    for f in range(F):
        prec_col = jnp.where(frow == f, prec_s[f], prec_col)
    sstack[0] = source_stack(mean_v[0], prec_col)
    loads["points"].wait()
    for j in range(W):
        cols = slice(j * TW, (j + 1) * TW)
        d = jnp.exp2(tdot(sstack[0], target_stack(points_v[:, cols])))
        dens[:, cols] = d
        colpart[j] = jnp.sum(d, axis=0, keepdims=True)
    load(5, "values", values_h, values_v)
    load(6, "cash", cash_h, cash_v)
    load(7, "salvage", salvage_h, salvage_v)
    load(8, "cost", cost_h, cost_v)

    loads["cot"].wait()
    loads["dec"].wait()
    cot = cot_v[...]
    dec = dec_v[...]
    adj[0] = jnp.where(dec == 0, cot, 0.0) + pair_swap(jnp.where(dec == 1, cot, 0.0))

    pl.semaphore_wait(barrier, len(peers))
    far = Z > 2 * NEAR + 1
    if far:
        for i in (NEAR, -NEAR):
            pl.semaphore_signal(far_sem, inc=1, device_id=at_z(i), device_id_type=MESH)

    sends = []
    rs = []
    for i, k in plane:
        n = i * C + k
        rs.append(remote(colpart.at[place(i, k)], rs_buf.at[n], rs_send.at[n], rs_recv.at[n], at_w(i, k)))
    sends += rs

    gathers = {}
    for i in near_y:
        gathers[i] = [
            remote(mean_v.at[0], mean_v.at[i], g_send.at[i, 0], g_recv.at[i, 0], at_w(i, 0)),
            remote(adj.at[0], adj.at[i], g_send.at[i, 1], g_recv.at[i, 1], at_w(i, 0)),
        ]
        sends += gathers[i]

    width = min(128, Z * R)
    lane = lax.broadcasted_iota(jnp.int32, (F, width), 1)
    per = width // R
    for half in range(2):
        core = (c + 1 + half) % C
        blocks = []
        for g in range(Z // per):
            block = jnp.zeros((F, width), F32)
            for k in range(per):
                off = (g * per + k) * (W * R) + (y * C + core) * R
                base = pl.multiple_of(off // width * width, width)
                turn = (k * R + width - off % width) % width
                piece = pltpu.roll(points_v[:, pl.ds(base, width)], turn, 1)
                block = jnp.where((lane >= k * R) & (lane < (k + 1) * R), piece, block)
            blocks.append(block)
        t2[half] = target_stack(jnp.concatenate(blocks, axis=1))

    def back_block(i, half, first):
        d = jnp.exp2(tdot(t2[half], sstack[i]))
        hi, lo = split2(d)
        a = beside(adj[i])
        term = dot(hi, a) + dot(lo, a)
        acc[half] = term if first else acc[half] + term

    back_block(0, 0, True)
    back_block(0, 1, True)

    loads["values"].wait()
    for j in range(W):
        rows = slice(j * TW, (j + 1) * TW)
        vstack[rows, :] = beside(values_v[rows, :])

    for cp in rs:
        cp.wait_recv()
    total = colpart[w]
    for i, k in plane:
        total = total + rs_buf[i * C + k]
    zc_src[...] = total
    zc_buf[0] = total
    if far:
        pl.semaphore_wait(far_sem, 2)
    zc = []
    for i in far_first(Z):
        zc.append(remote(zc_src, zc_buf.at[i], zc_send.at[i], zc_recv.at[i], at_z(i)))
    sends += zc

    for n, i in enumerate(near_y):
        for cp in gathers[i]:
            cp.wait_recv()
        sstack[i] = source_stack(mean_v[i], prec_col)
        back_block(i, 0, False)
        if n == len(near_y) - 1:
            sib_src[...] = acc[0, :, :M] + acc[0, :, M:]
            sib = remote(sib_src, sib_buf, sib_send, sib_recv, at_w(0, 1))
            sends.append(sib)
        back_block(i, 1, False)
    own_v[...] = acc[1, :, :M] + acc[1, :, M:]
    sib.wait_recv()

    for o in range(Z):
        for side in range(2):
            half = (z + side) % 2
            rows = pl.ds(pl.multiple_of(((z + o) % Z) * R + half * (R // 2), R // 2), R // 2)
            z_src[side, o] = own_v[rows, :] + sib_buf[rows, :]
    z1 = [
        remote(z_src.at[0, pl.ds(1, H)], z1_buf.at[1], z1_send.at[0], z1_recv.at[1], at_z(1)),
        remote(z_src.at[1, pl.ds(Z - H, H)], z1_buf.at[0], z1_send.at[1], z1_recv.at[0], at_z(-1)),
    ]
    sends += z1

    for cp in zc:
        cp.wait_recv()
    total = zc_buf[0]
    for i in range(1, Z):
        total = total + zc_buf[i]
    col_all[w] = total
    ag = {}
    for i, k in plane:
        n = i * C + k
        ag[i, k] = remote(col_all.at[w], col_all.at[w], ag_send.at[n], ag_recv.at[n], at_w(i, k))
        sends.append(ag[i, k])

    def forward(chip, core):
        j = place(chip, core)
        cols = pl.ds(pl.multiple_of(j * TW, TW), TW)
        hi, lo = split2(dens[:, cols] * (scale / col_all[j]))
        v = vstack[cols, :]
        return dot(hi, v) + dot(lo, v)

    both = forward(0, 0)

    for cp in z1:
        cp.wait_recv()
    z2_src[0, 0] = z_src[0, 0] + z1_buf[0, H - 1]
    z2_src[1, 0] = z_src[1, 0] + z1_buf[1, 0]
    z2 = []
    for k in range(H - 1, 0, -1):
        z2_src[0, k] = z_src[0, Z - k] + z1_buf[0, H - 1 - k]
        z2_src[1, k] = z_src[1, k] + z1_buf[1, k]
        for side, dev in ((0, at_z(-k)), (1, at_z(k))):
            z2.append(
                remote(z2_src.at[side, k], z2_buf.at[side, k], z2_send.at[side, k], z2_recv.at[side, k], dev)
            )
    sends += z2

    for i, k in reversed(plane):
        ag[(Y - i) % Y, (C - k) % C].wait_recv()
        both = both + forward(i, k)

    xr_src[...] = (both[:, :M] + both[:, M:]).reshape(X, S4, M)
    xr = []
    for i in far_first(X):
        xr.append(remote(xr_src.at[(x + i) % X], xr_buf.at[i], xr_send.at[i], xr_recv.at[i], at_x(i)))
    sends += xr

    own_off = s * R
    win = min(128, TW)
    inner = own_off % TW
    base = pl.multiple_of(inner // win * win, win)
    line = col_all[own_off // TW, :, pl.ds(base, win)]
    r_iota = lax.broadcasted_iota(jnp.int32, (R, win), 0)
    l_iota = lax.broadcasted_iota(jnp.int32, (R, win), 1)
    own_sum = jnp.sum(jnp.where(l_iota == r_iota + inner % win, line, 0.0), axis=1, keepdims=True)
    own_factor = scale / own_sum

    loads["cash"].wait()
    loads["salvage"].wait()
    loads["cost"].wait()
    for cp in xr:
        cp.wait_recv()
    rows = pl.ds(pl.multiple_of(x * S4, S4), S4)
    hold = xr_src[x]
    for i in range(1, X):
        hold = hold + xr_buf[i]
    hold = hold + cash_v[rows, :]
    value_v[x] = jnp.maximum(jnp.maximum(hold, pair_swap(hold) - cost_v[...]), salvage_v[rows, :])
    xa = []
    for i in far_first(X):
        xa.append(remote(value_v.at[x], value_v.at[x], xa_send.at[i], xa_recv.at[i], at_x(i)))
    sends += xa

    for cp in z2:
        cp.wait_recv()
    parts = [z2_src[0, 0], z2_src[1, 0]]
    for k in range(1, H):
        parts[k % 2] = parts[k % 2] + z2_buf[0, k]
        parts[1 - k % 2] = parts[1 - k % 2] + z2_buf[1, k]
    for side in range(2):
        own_v[pl.ds(pl.multiple_of((z + side) % 2 * (R // 2), R // 2), R // 2), :] = parts[side]
    adjoint_out[0] = own_v[pl.ds(0, R), :] * own_factor

    for cp in xa:
        cp.wait_recv()
    value_out[...] = value_v[...].reshape(S, M)
    for cp in sends:
        cp.wait_send()


def on_device(dims, mean, points, precision, values, cash, salvage, cost, cot, dec):
    Z, Y, C, X = dims
    W = Y * C
    F, S = mean.shape
    T = points.shape[1]
    M = cot.shape[1]
    R, TW, K = T // (Z * W), T // W, 7 * F
    scale = float(S * Z * W) / float(T * X)
    hbm = pl.BlockSpec(memory_space=pltpu.HBM)
    vmem = pl.BlockSpec(memory_space=pltpu.VMEM)
    dma = pltpu.SemaphoreType.DMA
    H = Z // 2
    scratch = [
        pltpu.VMEM((Y, F, S), F32), pltpu.VMEM((Y, S, M), F32), pltpu.VMEM((S, M), F32), pltpu.VMEM((S, M), jnp.int32),
        pltpu.VMEM((F, T), F32), pltpu.VMEM((T, M), F32), pltpu.VMEM((S, M), F32), pltpu.VMEM((S, M), F32),
        pltpu.SMEM((F,), F32), pltpu.VMEM((1, M), F32),
        pltpu.VMEM((S, T), F32), pltpu.VMEM((Y, K, S), BF16), pltpu.VMEM((2, K, Z * R), BF16),
        pltpu.VMEM((T, 2 * M), BF16), pltpu.VMEM((2, Z * R, 2 * M), F32),
        pltpu.VMEM((W, 1, TW), F32), pltpu.VMEM((W, 1, TW), F32), pltpu.VMEM((1, TW), F32), pltpu.VMEM((Z, 1, TW), F32),
        pltpu.VMEM((W, 1, TW), F32),
        pltpu.VMEM((Z * R, M), F32), pltpu.VMEM((Z * R, M), F32), pltpu.VMEM((Z * R, M), F32),
        pltpu.VMEM((2, Z, R // 2, M), F32), pltpu.VMEM((2, H, R // 2, M), F32),
        pltpu.VMEM((2, H, R // 2, M), F32), pltpu.VMEM((2, H, R // 2, M), F32),
        pltpu.VMEM((X, S // X, M), F32), pltpu.VMEM((X, S // X, M), F32), pltpu.VMEM((X, S // X, M), F32),
        dma((9,)), dma((Y, 2)), dma((Y, 2)), dma((W,)), dma((W,)), dma((Z,)), dma((Z,)), dma((W,)), dma((W,)),
        dma, dma, dma((2,)), dma((2,)), dma((2, H)), dma((2, H)), dma((X,)), dma((X,)), dma((X,)), dma((X,)),
        pltpu.SemaphoreType.REGULAR,
    ]
    return pl.pallas_call(
        functools.partial(kernel, dims, scale),
        out_shape=(jax.ShapeDtypeStruct((S, M), F32), jax.ShapeDtypeStruct((1, R, M), F32)),
        in_specs=[hbm] * 9,
        out_specs=(vmem, vmem),
        scratch_shapes=scratch,
        compiler_params=pltpu.CompilerParams(
            collective_id=0, has_side_effects=True, vmem_limit_bytes=60 * 1024 * 1024
        ),
        name="mesh_step",
    )(mean, points, precision, values, cash, salvage, cost.reshape(1, M), cot, dec)


def build(mesh, dims):
    placed = (
        P(None, "src"), P(None, "tgt"), P(), P("tgt", None), P("src", None), P("src", None), P(), P("src", None),
        P("src", None),
    )
    return jax.shard_map(
        functools.partial(on_device, dims),
        mesh=mesh,
        in_specs=placed,
        out_specs=(P("src", None), P("tgt", "src", None)),
        check_vma=False,
    )


def solution(mesh):
    src, tgt = mesh.shape["src"], mesh.shape["tgt"]
    return build(mesh, (src // 8, 4, 2, tgt))
```

time: 55.4 us -> 44.1 us (0.80)
  Pallas kernels: 51.7 us -> 40.3 us
    pallas_call x1, Pallas kernels: 51.7 us -> 40.3 us  [on_device(): pl.pallas_call(functools.partial(kernel, dims, scale), out_shape=(jax.Sha...]
where the time goes in v2:
time: 44.1 us; the launch traced here: 43.9 us
  Pallas kernels  40.3 us (91%)
  local copies, waits for them, and re-layouts  2.89 us (7%)
  between operations  0.64 us (1%)
    pallas_call x1, Pallas kernels, on_device(): pl.pallas_call(functools.partial(kernel, dims, scale), out_shape=(jax.Sha...  40.3 us
    unnamed x2, local copies, waits for them, and re-layouts  2.89 us

profile of v2, /device:TPU:1, one launch (start us, length us, event | category | flops | bytes accessed | tf_op | source)
XLA Modules:
  0.0 43.9 jit_solution(11301498375100963190)
XLA Ops:
  0.6 40.3 %mesh_step.1 = (f32[256,128]{1,0:T(8,128)}, f32[1,32,128]{2,1,0:T(8,128)}) custom-call(f32[16,256]{1,0:T(8,128)} %mean_h.1, f32[16,4096]{1,0:T(8,128)} %points_h.1, f32[16]{0:T(128)} %prec_h.1, f32[4096,128]{1,0:T(8,128)} %values_h.1, f32[256,128]{1,0:T(8,128)} %cash_h.1, f32[256,128]{1,0:T(8,128)} %salvage_h.1, f32[1,128]{1,0:T(1,128)} %bitcast.1, ...), custom_call_target="tpu_custom_call" | custom-call | tf_op jit(solution)/shard_map/mesh_step/pallas_call | solution.py:367
  41.0 1.6 %copy.13 = f32[256,128]{1,0:T(8,128)} copy(f32[256,128]{1,0:T(8,128)} %get-tuple-element.4) | data formatting | bytes 262144
  42.6 1.3 %copy.14 = f32[1,32,128]{2,1,0:T(8,128)} copy(f32[1,32,128]{2,1,0:T(8,128)} %get-tuple-element.5) | data formatting | bytes 32768

commit v3 on v2

--- a/solution.py
+++ b/solution.py
@@ -121,17 +121,17 @@
         loads[name] = pltpu.make_async_copy(src, dst, ld_sem.at[k])
         loads[name].start()
 
+    barrier = pltpu.get_barrier_semaphore()
+    near_z = [i for i in far_first(Z) if min(i, Z - i) <= NEAR]
+    peers = [at_z(i) for i in near_z] + [at_w(i, k) for i, k in plane] + [at_x(i) for i in far_first(X)]
+    for dev in peers:
+        pl.semaphore_signal(barrier, inc=1, device_id=dev, device_id_type=MESH)
+
     load(0, "prec", prec_h, prec_s)
     load(1, "mean", mean_h, mean_v.at[0])
     load(2, "points", points_h, points_v)
     load(3, "cot", cot_h, cot_v)
     load(4, "dec", dec_h, dec_v)
-
-    barrier = pltpu.get_barrier_semaphore()
-    near_z = [i for i in far_first(Z) if min(i, Z - i) <= NEAR]
-    peers = [at_z(i) for i in near_z] + [at_w(i, k) for i, k in plane] + [at_x(i) for i in far_first(X)]
-    for dev in peers:
-        pl.semaphore_signal(barrier, inc=1, device_id=dev, device_id_type=MESH)
 
     loads["prec"].wait()
     loads["mean"].wait()
@@ -235,6 +235,18 @@
             sends.append(sib)
         back_block(i, 1, False)
     own_v[...] = acc[1, :, :M] + acc[1, :, M:]
+    for cp in zc:
+        cp.wait_recv()
+    total = zc_buf[0]
+    for i in range(1, Z):
+        total = total + zc_buf[i]
+    col_all[w] = total
+    ag = {}
+    for i, k in plane:
+        n = i * C + k
+        ag[i, k] = remote(col_all.at[w], col_all.at[w], ag_send.at[n], ag_recv.at[n], at_w(i, k))
+        sends.append(ag[i, k])
+
     sib.wait_recv()
 
     for o in range(Z):
@@ -248,18 +260,6 @@
     ]
     sends += z1
 
-    for cp in zc:
-        cp.wait_recv()
-    total = zc_buf[0]
-    for i in range(1, Z):
-        total = total + zc_buf[i]
-    col_all[w] = total
-    ag = {}
-    for i, k in plane:
-        n = i * C + k
-        ag[i, k] = remote(col_all.at[w], col_all.at[w], ag_send.at[n], ag_recv.at[n], at_w(i, k))
-        sends.append(ag[i, k])
-
     def forward(chip, core):
         j = place(chip, core)
         cols = pl.ds(pl.multiple_of(j * TW, TW), TW)
@@ -268,6 +268,13 @@
         return dot(hi, v) + dot(lo, v)
 
     both = forward(0, 0)
+
+    def forward_from(i, k):
+        ag[(Y - i) % Y, (C - k) % C].wait_recv()
+        return forward(i, k)
+
+    for i, k in reversed(plane[C:]):
+        both = both + forward_from(i, k)
 
     for cp in z1:
         cp.wait_recv()
@@ -283,9 +290,8 @@
             )
     sends += z2
 
-    for i, k in reversed(plane):
-        ag[(Y - i) % Y, (C - k) % C].wait_recv()
-        both = both + forward(i, k)
+    for i, k in plane[:C]:
+        both = both + forward_from(i, k)
 
     xr_src[...] = (both[:, :M] + both[:, M:]).reshape(X, S4, M)
     xr = []
@@ -334,6 +340,17 @@
     value_out[...] = value_v[...].reshape(S, M)
     for cp in sends:
         cp.wait_send()
+
+
+def place_results(value_in, adjoint_in, value_out, adjoint_out, sem):
+    copies = [
+        pltpu.make_async_copy(value_in, value_out, sem.at[0]),
+        pltpu.make_async_copy(adjoint_in, adjoint_out, sem.at[1]),
+    ]
+    for cp in copies:
+        cp.start()
+    for cp in copies:
+        cp.wait()
 
 
 def on_device(dims, mean, points, precision, values, cash, salvage, cost, cot, dec):
@@ -364,9 +381,11 @@
         dma, dma, dma((2,)), dma((2,)), dma((2, H)), dma((2, H)), dma((X,)), dma((X,)), dma((X,)), dma((X,)),
         pltpu.SemaphoreType.REGULAR,
     ]
-    return pl.pallas_call(
+    shapes = (jax.ShapeDtypeStruct((S, M), F32), jax.ShapeDtypeStruct((1, R, M), F32))
+    held = (pltpu.VMEM((S, M), F32), pltpu.VMEM((1, R, M), F32))
+    results = pl.pallas_call(
         functools.partial(kernel, dims, scale),
-        out_shape=(jax.ShapeDtypeStruct((S, M), F32), jax.ShapeDtypeStruct((1, R, M), F32)),
+        out_shape=held,
         in_specs=[hbm] * 9,
         out_specs=(vmem, vmem),
         scratch_shapes=scratch,
@@ -375,6 +394,7 @@
         ),
         name="mesh_step",
     )(mean, points, precision, values, cash, salvage, cost.reshape(1, M), cot, dec)
+    return results
 
 
 def build(mesh, dims):

time: 44.1 us -> 40.6 us (0.921)
  Pallas kernels: 40.3 us -> 38.6 us
  local copies, waits for them, and re-layouts: 2.89 us -> 1.26 us
    pallas_call x1, Pallas kernels: 40.3 us -> 38.6 us  [on_device(): pl.pallas_call(functools.partial(kernel, dims, scale), out_shape=held, in...]
    unnamed x2, local copies, waits for them, and re-layouts: 2.89 us -> 1.26 us
where the time goes in v3:
time: 40.6 us; the launch traced here: 40.5 us
  Pallas kernels  38.6 us (95%)
  local copies, waits for them, and re-layouts  1.26 us (3%)
  between operations  0.64 us (2%)
    pallas_call x1, Pallas kernels, on_device(): pl.pallas_call(functools.partial(kernel, dims, scale), out_shape=held, in...  38.6 us
    unnamed x2, local copies, waits for them, and re-layouts  1.26 us

profile of v3, /device:TPU:1, one launch (start us, length us, event | category | flops | bytes accessed | tf_op | source)
XLA Modules:
  0.0 40.5 jit_solution(13671925255961745845)
XLA Ops:
  0.6 38.6 %mesh_step.1 = (f32[256,128]{1,0:T(8,128)S(1)}, f32[1,32,128]{2,1,0:T(8,128)S(1)}) custom-call(f32[16,256]{1,0:T(8,128)} %mean_h.1, f32[16,4096]{1,0:T(8,128)} %points_h.1, f32[16]{0:T(128)} %prec_h.1, f32[4096,128]{1,0:T(8,128)} %values_h.1, f32[256,128]{1,0:T(8,128)} %cash_h.1, f32[256,128]{1,0:T(8,128)} %salvage_h.1, f32[1,128]{1,0:T(1,128)} %bitcast.1, ...), custom_call_target="tpu_custom_call" | custom-call | tf_op jit(solution)/shard_map/mesh_step/pallas_call | solution.py:386
  39.2 0.7 %copy.13 = f32[256,128]{1,0:T(8,128)} copy(f32[256,128]{1,0:T(8,128)S(1)} %get-tuple-element.2) | data formatting | bytes 262144
  39.9 0.6 %copy.14 = f32[1,32,128]{2,1,0:T(8,128)} copy(f32[1,32,128]{2,1,0:T(8,128)S(1)} %get-tuple-element.3) | data formatting | bytes 32768

commit v4 on v3

--- a/solution.py
+++ b/solution.py
@@ -74,7 +74,7 @@
     sib_src, sib_buf, own_v, z_src, z1_buf, z2_src, z2_buf,
     xr_src, xr_buf, value_v,
     ld_sem, g_send, g_recv, rs_send, rs_recv, zc_send, zc_recv, ag_send, ag_recv,
-    sib_send, sib_recv, z1_send, z1_recv, z2_send, z2_recv, xr_send, xr_recv, xa_send, xa_recv, far_sem,
+    sib_send, sib_recv, z1_send, z1_recv, z2_send, z2_recv, xr_send, xr_recv, xa_send, xa_recv, plane_sem, far_sem,
 ):
     Z, Y, C, X = dims
     W = Y * C
@@ -84,7 +84,6 @@
     R = T // (Z * W)
     S4 = S // X
     H = Z // 2
-    NEAR = 4
     s = lax.axis_index("src")
     x = lax.axis_index("tgt")
     z, w = s // W, s % W
@@ -122,16 +121,23 @@
         loads[name].start()
 
     barrier = pltpu.get_barrier_semaphore()
-    near_z = [i for i in far_first(Z) if min(i, Z - i) <= NEAR]
-    peers = [at_z(i) for i in near_z] + [at_w(i, k) for i, k in plane] + [at_x(i) for i in far_first(X)]
-    for dev in peers:
-        pl.semaphore_signal(barrier, inc=1, device_id=dev, device_id_type=MESH)
+    def told(zz, yy, cc, xx):
+        pl.semaphore_signal(barrier, inc=1, device_id=((zz * Y + yy) * C + cc, xx), device_id_type=MESH)
+
+    for i in reversed(near_y):
+        told(z, (y + i) % Y, 1, x)
+    for i in far_first(X):
+        told(z, y, 1, (x + i) % X)
+    told(z, y, 1 - c, x)
 
     load(0, "prec", prec_h, prec_s)
     load(1, "mean", mean_h, mean_v.at[0])
     load(2, "points", points_h, points_v)
     load(3, "cot", cot_h, cot_v)
     load(4, "dec", dec_h, dec_v)
+
+    for i in far_first(Z):
+        told((z + i) % Z, y, 0, x)
 
     loads["prec"].wait()
     loads["mean"].wait()
@@ -157,11 +163,14 @@
     dec = dec_v[...]
     adj[0] = jnp.where(dec == 0, cot, 0.0) + pair_swap(jnp.where(dec == 1, cot, 0.0))
 
-    pl.semaphore_wait(barrier, len(peers))
-    far = Z > 2 * NEAR + 1
-    if far:
-        for i in (NEAR, -NEAR):
-            pl.semaphore_signal(far_sem, inc=1, device_id=at_z(i), device_id_type=MESH)
+    @pl.when(c == 1)
+    def _():
+        pl.semaphore_wait(barrier, 2 * (Y - 1) + 2 * (X - 1) + 1)
+        pl.semaphore_signal(plane_sem, inc=1, device_id=at_w(0, 1), device_id_type=MESH)
+
+    @pl.when(c == 0)
+    def _():
+        pl.semaphore_wait(plane_sem, 1)
 
     sends = []
     rs = []
@@ -210,6 +219,11 @@
         rows = slice(j * TW, (j + 1) * TW)
         vstack[rows, :] = beside(values_v[rows, :])
 
+    @pl.when(c == 0)
+    def _():
+        pl.semaphore_wait(barrier, 2 * (Z - 1) + 1)
+        pl.semaphore_signal(far_sem, inc=1, device_id=at_w(0, 1), device_id_type=MESH)
+
     for cp in rs:
         cp.wait_recv()
     total = colpart[w]
@@ -217,8 +231,10 @@
         total = total + rs_buf[i * C + k]
     zc_src[...] = total
     zc_buf[0] = total
-    if far:
-        pl.semaphore_wait(far_sem, 2)
+    @pl.when(c == 1)
+    def _():
+        pl.semaphore_wait(far_sem, 1)
+
     zc = []
     for i in far_first(Z):
         zc.append(remote(zc_src, zc_buf.at[i], zc_send.at[i], zc_recv.at[i], at_z(i)))
@@ -276,6 +292,16 @@
     for i, k in reversed(plane[C:]):
         both = both + forward_from(i, k)
 
+    for i, k in plane[:C]:
+        both = both + forward_from(i, k)
+
+    xr_src[...] = (both[:, :M] + both[:, M:]).reshape(X, S4, M)
+    xr = []
+    for i in far_first(X):
+        xr.append(remote(xr_src.at[(x + i) % X], xr_buf.at[i], xr_send.at[i], xr_recv.at[i], at_x(i)))
+    for cp in sends:
+        cp.wait_send()
+
     for cp in z1:
         cp.wait_recv()
     z2_src[0, 0] = z_src[0, 0] + z1_buf[0, H - 1]
@@ -290,15 +316,6 @@
             )
     sends += z2
 
-    for i, k in plane[:C]:
-        both = both + forward_from(i, k)
-
-    xr_src[...] = (both[:, :M] + both[:, M:]).reshape(X, S4, M)
-    xr = []
-    for i in far_first(X):
-        xr.append(remote(xr_src.at[(x + i) % X], xr_buf.at[i], xr_send.at[i], xr_recv.at[i], at_x(i)))
-    sends += xr
-
     own_off = s * R
     win = min(128, TW)
     inner = own_off % TW
@@ -323,7 +340,8 @@
     xa = []
     for i in far_first(X):
         xa.append(remote(value_v.at[x], value_v.at[x], xa_send.at[i], xa_recv.at[i], at_x(i)))
-    sends += xa
+    for cp in xr + z2:
+        cp.wait_send()
 
     for cp in z2:
         cp.wait_recv()
@@ -338,7 +356,7 @@
     for cp in xa:
         cp.wait_recv()
     value_out[...] = value_v[...].reshape(S, M)
-    for cp in sends:
+    for cp in xa:
         cp.wait_send()
 
 
@@ -379,7 +397,7 @@
         pltpu.VMEM((X, S // X, M), F32), pltpu.VMEM((X, S // X, M), F32), pltpu.VMEM((X, S // X, M), F32),
         dma((9,)), dma((Y, 2)), dma((Y, 2)), dma((W,)), dma((W,)), dma((Z,)), dma((Z,)), dma((W,)), dma((W,)),
         dma, dma, dma((2,)), dma((2,)), dma((2, H)), dma((2, H)), dma((X,)), dma((X,)), dma((X,)), dma((X,)),
-        pltpu.SemaphoreType.REGULAR,
+        pltpu.SemaphoreType.REGULAR, pltpu.SemaphoreType.REGULAR,
     ]
     shapes = (jax.ShapeDtypeStruct((S, M), F32), jax.ShapeDtypeStruct((1, R, M), F32))
     held = (pltpu.VMEM((S, M), F32), pltpu.VMEM((1, R, M), F32))

time: 40.6 us -> 39.9 us (0.983)
  Pallas kernels: 38.6 us -> 37.8 us
    pallas_call x1, Pallas kernels: 38.6 us -> 37.8 us  [on_device(): pl.pallas_call(functools.partial(kernel, dims, scale), out_shape=held, in...]
where the time goes in v4:
time: 39.9 us; the launch traced here: 39.7 us
  Pallas kernels  37.8 us (95%)
  local copies, waits for them, and re-layouts  1.26 us (3%)
  between operations  0.64 us (2%)
    pallas_call x1, Pallas kernels, on_device(): pl.pallas_call(functools.partial(kernel, dims, scale), out_shape=held, in...  37.8 us
    unnamed x2, local copies, waits for them, and re-layouts  1.26 us

profile of v4, /device:TPU:1, one launch (start us, length us, event | category | flops | bytes accessed | tf_op | source)
XLA Modules:
  0.0 39.7 jit_solution(8213327464879342916)
XLA Ops:
  0.6 37.8 %mesh_step.1 = (f32[256,128]{1,0:T(8,128)S(1)}, f32[1,32,128]{2,1,0:T(8,128)S(1)}) custom-call(f32[16,256]{1,0:T(8,128)} %mean_h.1, f32[16,4096]{1,0:T(8,128)} %points_h.1, f32[16]{0:T(128)} %prec_h.1, f32[4096,128]{1,0:T(8,128)} %values_h.1, f32[256,128]{1,0:T(8,128)} %cash_h.1, f32[256,128]{1,0:T(8,128)} %salvage_h.1, f32[1,128]{1,0:T(1,128)} %bitcast.1, ...), custom_call_target="tpu_custom_call" | custom-call | tf_op jit(solution)/shard_map/mesh_step/pallas_call | solution.py:404
  38.5 0.7 %copy.13 = f32[256,128]{1,0:T(8,128)} copy(f32[256,128]{1,0:T(8,128)S(1)} %get-tuple-element.2) | data formatting | bytes 262144
  39.1 0.6 %copy.14 = f32[1,32,128]{2,1,0:T(8,128)} copy(f32[1,32,128]{2,1,0:T(8,128)S(1)} %get-tuple-element.3) | data formatting | bytes 32768

commit v5 on v4

--- a/solution.py
+++ b/solution.py
@@ -299,9 +299,6 @@
     xr = []
     for i in far_first(X):
         xr.append(remote(xr_src.at[(x + i) % X], xr_buf.at[i], xr_send.at[i], xr_recv.at[i], at_x(i)))
-    for cp in sends:
-        cp.wait_send()
-
     for cp in z1:
         cp.wait_recv()
     z2_src[0, 0] = z_src[0, 0] + z1_buf[0, H - 1]
@@ -314,7 +311,9 @@
             z2.append(
                 remote(z2_src.at[side, k], z2_buf.at[side, k], z2_send.at[side, k], z2_recv.at[side, k], dev)
             )
-    sends += z2
+
+    for cp in sends:
+        cp.wait_send()
 
     own_off = s * R
     win = min(128, TW)

time: 39.9 us -> 39.9 us (level)
  no operation moved by 1% of the time
where the time goes in v5:
time: 39.9 us; the launch traced here: 39.7 us
  Pallas kernels  37.8 us (95%)
  local copies, waits for them, and re-layouts  1.26 us (3%)
  between operations  0.64 us (2%)
    pallas_call x1, Pallas kernels, on_device(): pl.pallas_call(functools.partial(kernel, dims, scale), out_shape=held, in...  37.8 us
    unnamed x2, local copies, waits for them, and re-layouts  1.26 us

profile of v5, /device:TPU:1, one launch (start us, length us, event | category | flops | bytes accessed | tf_op | source)
XLA Modules:
  0.0 39.7 jit_solution(17677963344580296819)
XLA Ops:
  0.6 37.8 %mesh_step.1 = (f32[256,128]{1,0:T(8,128)S(1)}, f32[1,32,128]{2,1,0:T(8,128)S(1)}) custom-call(f32[16,256]{1,0:T(8,128)} %mean_h.1, f32[16,4096]{1,0:T(8,128)} %points_h.1, f32[16]{0:T(128)} %prec_h.1, f32[4096,128]{1,0:T(8,128)} %values_h.1, f32[256,128]{1,0:T(8,128)} %cash_h.1, f32[256,128]{1,0:T(8,128)} %salvage_h.1, f32[1,128]{1,0:T(1,128)} %bitcast.1, ...), custom_call_target="tpu_custom_call" | custom-call | tf_op jit(solution)/shard_map/mesh_step/pallas_call | solution.py:403
  38.5 0.7 %copy.13 = f32[256,128]{1,0:T(8,128)} copy(f32[256,128]{1,0:T(8,128)S(1)} %get-tuple-element.2) | data formatting | bytes 262144
  39.1 0.6 %copy.14 = f32[1,32,128]{2,1,0:T(8,128)} copy(f32[1,32,128]{2,1,0:T(8,128)S(1)} %get-tuple-element.3) | data formatting | bytes 32768
